TPU v7x, 32 devices: a whole 2x2x4 slice. The times are simulated.
32 devices in a mesh: req: 16 (over z, x, core), blk: 2 (over y).
Axes of the slice: x: 2, y: 2, z: 4, core: 2. Of those that a mesh axis runs over, the one named last changes fastest.
Arguments:
- queries: bfloat16 [32, 64, 2048], P('req', 'blk'), may hold values from -5 to 5
- cache_keys: bfloat16 [32, 1024, 2048], P('req', 'blk'), may hold values from -5 to 5
- cache_values: bfloat16 [32, 1024, 2048], P('req', 'blk'), may hold values from -6 to 6
- draft_keys: bfloat16 [32, 64, 2048], P('req', 'blk'), may hold values from -6 to 6
- draft_values: bfloat16 [32, 64, 2048], P('req', 'blk'), may hold values from -6 to 6
- parents: int32 [32, 64], P('req'), may hold values from -1 to 62, as said below
- lengths: int32 [32], P('req'), may hold values from 2 to 1024
- out_weight: bfloat16 [2048, 4096], P('req'), may hold values from -0.125 to 0.125
Outputs:
- mixed: bfloat16 [32, 64, 4096], P('req', 'blk')
Inputs may be any that keep to these rules, and one draw needn't show every extreme that they name: parents[r, t] is below t; parents[r, 0] = -1 marks the root, which follows the cache.
All inputs are finite; a program needn't handle non-finite values.
Results may differ from a plain program's by a relative error of at most 0.0054.
Values may be sent and summed in bfloat16 or wider, within the bound.
A program may use at most 128 MiB of HBM per device.

v0:
```python
import jax
import jax.numpy as jnp
from jax import lax
from jax.sharding import PartitionSpec as P

HEAD = 128
HEADS = 16


def ancestors(parent_row):
    count = parent_row.shape[0]
    index = jnp.arange(count)
    links = (parent_row[:, None] == index[None, :]).astype(jnp.float32)
    links = links + (index[:, None] == index[None, :]).astype(jnp.float32)
    for _ in range(count.bit_length()):
        links = jnp.minimum(
            jnp.dot(
                links, links, precision=lax.Precision.HIGHEST, preferred_element_type=jnp.float32
            ),
            1.0,
        )
    return links > 0.5


def shards(
    queries, cache_keys, cache_values, draft_keys, draft_values, parents, lengths, out_weight
):
    batch, own_tokens, width = queries.shape
    keys_dev = cache_keys.shape[1]
    scale = HEAD ** (-0.5)
    position = lax.axis_index("blk")
    whole_q = lax.all_gather(queries, "blk", axis=1, tiled=True)
    tree = whole_q.shape[1]
    query_heads = whole_q.reshape(batch, tree, HEADS, HEAD)
    cache_kh = cache_keys.reshape(batch, keys_dev, HEADS, HEAD)
    cache_vh = cache_values.reshape(batch, keys_dev, HEADS, HEAD)
    draft_kh = draft_keys.reshape(batch, own_tokens, HEADS, HEAD)
    draft_vh = draft_values.reshape(batch, own_tokens, HEADS, HEAD)
    cache_scores = (
        jnp.einsum("rthe,rkhe->rhtk", query_heads, cache_kh, preferred_element_type=jnp.float32)
        * scale
    )
    slots = position * keys_dev + jnp.arange(keys_dev)
    cache_seen = (slots[None, :] < lengths[:, None])[:, None, None, :]
    cache_scores = jnp.where(cache_seen, cache_scores, -1e30)
    lineage = jax.vmap(ancestors)(parents)
    own_lineage = lax.dynamic_slice_in_dim(lineage, position * own_tokens, own_tokens, 2)[:, None]
    tree_scores = (
        jnp.einsum("rthe,rshe->rhts", query_heads, draft_kh, preferred_element_type=jnp.float32)
        * scale
    )
    tree_scores = jnp.where(own_lineage, tree_scores, -1e30)
    local_max = jnp.maximum(jnp.max(cache_scores, axis=-1), jnp.max(tree_scores, axis=-1))
    row_max = lax.pmax(local_max, "blk")
    cache_weights = jnp.where(cache_seen, jnp.exp(cache_scores - row_max[..., None]), 0.0)
    tree_weights = jnp.where(own_lineage, jnp.exp(tree_scores - row_max[..., None]), 0.0)
    totals = jnp.transpose(
        jnp.sum(cache_weights, axis=-1) + jnp.sum(tree_weights, axis=-1), (0, 2, 1)
    )
    numer = jnp.einsum(
        "rhtk,rkhe->rthe",
        cache_weights.astype(jnp.bfloat16),
        cache_vh,
        preferred_element_type=jnp.float32,
    )
    numer = numer + jnp.einsum(
        "rhts,rshe->rthe",
        tree_weights.astype(jnp.bfloat16),
        draft_vh,
        preferred_element_type=jnp.float32,
    )
    numer = numer.reshape(batch, tree, width)
    summed_numer, summed_totals = lax.psum((numer, totals), "blk")
    own_numer = lax.dynamic_slice_in_dim(summed_numer, position * own_tokens, own_tokens, 1)
    own_totals = lax.dynamic_slice_in_dim(summed_totals, position * own_tokens, own_tokens, 1)
    attended = own_numer.reshape(batch, own_tokens, HEADS, HEAD) / own_totals[..., None]
    attended = attended.reshape(batch, own_tokens, width).astype(jnp.bfloat16)
    mixed = jnp.einsum(
        "rtc,cd->rtd",
        attended,
        lax.all_gather(out_weight, "req", axis=0, tiled=True),
        preferred_element_type=jnp.float32,
    )
    return mixed.astype(jnp.bfloat16)


def solution(mesh):
    in_specs = (
        P("req", "blk", None),
        P("req", "blk", None),
        P("req", "blk", None),
        P("req", "blk", None),
        P("req", "blk", None),
        P("req", None),
        P("req"),
        P("req", None),
    )
    out_specs = P("req", "blk", None)
    return jax.shard_map(shards, mesh=mesh, in_specs=in_specs, out_specs=out_specs, check_vma=False)
```

profile of v0, /device:TPU:0, one launch (start us, length us, event | category | flops | bytes accessed | tf_op | source)
XLA Modules:
  0.0 189.3 jit_solution(2522333886554143752)
XLA Ops:
  7.4 1.0 convolution_minimum_fusion.5
  8.4 0.2 convolution_minimum_fusion.4
  8.6 0.2 convolution_minimum_fusion.3
  8.8 0.2 convolution_minimum_fusion.2
  9.0 0.2 convolution_minimum_fusion.1
  9.2 0.2 convolution_minimum_fusion
  9.4 0.2 fusion.48
  9.6 0.1 fusion.36
  9.8 10.2 %all_gather.6 = bf16[2,64,2048]{2,1,0:T(8,128)(2,1)S(1)} all-gather(bf16[2,32,2048]{2,1,0:T(8,128)(2,1)} %param.8), channel_id=1, replica_groups=mesh['req'=16,'blk'=2] {'blk'}, dimensions={1}, use_global_device_ids=true | all-gather | bytes 786432 | tf_op jit(solution)/shard_map/all_gather | solution.py:32
  20.0 0.7 broadcast_compare_fusion
  20.7 1.4 fusion.47
  22.1 5.7 %fusion.11 = (f32[2,16,64]{2,1,0:T(8,128)S(1)}, f32[2,16,64,512]{3,2,1,0:T(8,128)}) fusion(pred[2,512]{1,0:T(4,128)(4,1)S(1)} %broadcast_compare_fusion, bf16[2,512,2048]{2,1,0:T(8,128)(2,1)} %param.9, bf16[2,64,2048]{2,1,0:T(8,128)(2,1)S(1)} %all_gather.6), kind=kOutput, calls=%fused_computation.11 | convolution fusion | flops 271579136 | bytes 8922112 | tf_op jit(solution)/shard_map/rthe,rkhe->rhtk/dot_general | solution.py:40
  27.8 8.3 %pmax.7 = f32[2,16,64]{2,1,0:T(8,128)S(1)} all-reduce(f32[2,16,64]{2,1,0:T(8,128)S(1)} %max.5), channel_id=1, replica_groups=mesh['req'=16,'blk'=2] {'blk'}, use_global_device_ids=true, to_apply=%region_2.3 | all-reduce | flops 2048 | bytes 16384 | tf_op jit(solution)/shard_map/pmax | solution.py:54
  36.2 5.0 %fusion.5 = f32[2,16,64,128]{3,2,1,0:T(8,128)S(1)} fusion(f32[2,16,64,512]{3,2,1,0:T(8,128)} %get-tuple-element.6, f32[2,16,64]{2,1,0:T(8,128)S(1)} %pmax.7, pred[2,512]{1,0:T(4,128)(4,1)S(1)} %broadcast_compare_fusion, bf16[2,512,2048]{2,1,0:T(8,128)(2,1)} %param.10), kind=kOutput, calls=%fused_computation.3 | convolution fusion | flops 273678336 | bytes 9446400 | tf_op jit(solution)/shard_map/rhtk,rkhe->rthe/dot_general | solution.py:60
  41.2 0.3 fusion.20
  41.5 1.1 copy.74
  42.7 0.5 all-gather.2.cloned.1.call-update
  43.3 0.1 fusion.26
  43.4 3.4 %fusion.12 = f32[2,16,64]{2,1,0:T(8,128)S(1)} fusion(f32[2,16,64,512]{3,2,1,0:T(8,128)} %get-tuple-element.6, f32[2,16,64]{2,1,0:T(8,128)S(1)} %pmax.7, pred[2,512]{1,0:T(4,128)(4,1)S(1)} %broadcast_compare_fusion), kind=kLoop, calls=%fused_computation.12 | loop fusion | flops 5240832 | bytes 4211712 | tf_op jit(solution)/shard_map/reduce_sum | solution.py:58
  46.8 7.1 %psum.15 = f32[2,64,16]{1,2,0:T(8,128)S(1)} all-reduce(f32[2,64,16]{1,2,0:T(8,128)S(1)} %add_bitcast_fusion), channel_id=1, replica_groups=mesh['req'=16,'blk'=2] {'blk'}, use_global_device_ids=true, to_apply=%region_6.7 | all-reduce | flops 2048 | bytes 16384 | tf_op jit(solution)/shard_map/psum | solution.py:73
  54.1 0.2 div.11
  54.4 29.0 %all-reduce.2.cloned.1.call-done = f32[2,64,2048]{2,1,0:T(8,128)} async-done(((f32[2,64,2048]{2,1,0:T(8,128)}), f32[2,64,2048]{2,1,0:T(8,128)}) %all-reduce.2.cloned.1.call-update) | async-done | bytes 1048592 | tf_op jit(solution)/shard_map/psum | solution.py:73
  83.4 88.7 %all-gather.2.cloned.1.call-done = bf16[2048,4096]{1,0:T(8,128)(2,1)} async-done(((bf16[128,4096]{1,0:T(8,128)(2,1)}), bf16[2048,4096]{1,0:T(8,128)(2,1)}) %all-gather.2.cloned.1.call-update) | async-done | bytes 16777232 | tf_op jit(solution)/shard_map/all_gather | solution.py:81
  172.1 9.8 %fusion.2 = bf16[2,32,4096]{2,1,0:T(8,128)(2,1)} fusion(bf16[2048,4096]{1,0:T(8,128)(2,1)} %all-gather.2.cloned.1.call-done, f32[2,32,2048]{2,1,0:T(8,128)S(1)} %div.12, f32[2,64,2048]{2,1,0:T(8,128)} %all-reduce.2.cloned.1.call-done, s32[]{:T(128)S(6)} %select_n.20), kind=kOutput, calls=%fused_computation.2 | convolution fusion | flops 1074266112 | bytes 18350084 | tf_op jit(solution)/shard_map/rtc,cd->rtd/dot_general | solution.py:78
  (13 shorter events, 0.4 us)
Async XLA Ops:
  7.4 33.8 %copy-start = (bf16[2,32,2048]{2,1,0:T(8,128)(2,1)S(1)}, bf16[2,32,2048]{2,1,0:T(8,128)(2,1)}, u32[]{:S(2)}) copy-start(bf16[2,32,2048]{2,1,0:T(8,128)(2,1)} %param.12) | copy-start | bytes 786436
  7.4 76.0 %all-reduce.2.cloned.1.call-start = ((), (), s32[]{:S(2)}) async-start(), calls=%async_computation | async-start | bytes 2097152 | tf_op jit(solution)/shard_map/psum | solution.py:73
  42.7 129.4 %all-gather.2.cloned.1.call-start = ((), (), s32[]{:S(2)}) async-start(), calls=%async_computation.1 | async-start | bytes 17825792 | tf_op jit(solution)/shard_map/all_gather | solution.py:81
Sparse Core Ops, SparseCore 0:
  42.8 40.5 all-reduce.1
Sparse Core Ops, SparseCore 1:
  45.3 126.7 all-gather.1
where the time goes:
time: 190 us; the launch traced here: 189 us
  waiting for transfers between devices  118 us (62%)
  blocking collectives  25.7 us (14%)
  matrix products  24.4 us (13%)
  between operations  15 us (8%)
  other arithmetic  4.35 us (2%)
    all_gather x1, waiting for transfers between devices, shards(): lax.all_gather(out_weight, 'req', axis=0, tiled=True)  88.7 us
    psum x1, waiting for transfers between devices, shards(): summed_numer, summed_totals = lax.psum((numer, totals), 'blk')  29 us
    all_gather x1, blocking collectives, shards(): whole_q = lax.all_gather(queries, 'blk', axis=1, tiled=True)  10.2 us
    dot_general x1, matrix products, shards(): jnp.einsum('rtc,cd->rtd', attended, lax.all_gather(out_weight, 'req', axi...  9.77 us
    pmax x1, blocking collectives, shards(): row_max = lax.pmax(local_max, 'blk')  8.35 us
    psum x1, blocking collectives, shards(): summed_numer, summed_totals = lax.psum((numer, totals), 'blk')  7.14 us
    dot_general x1, matrix products, shards(): jnp.einsum('rthe,rkhe->rhtk', query_heads, cache_kh, preferred_element_ty...  5.72 us
    dot_general x1, matrix products, shards(): jnp.einsum('rhtk,rkhe->rthe', cache_weights.astype(jnp.bfloat16), cache_v...  4.98 us
  transfers between devices with their start and end apart: 2, of which 2 were waited for; matrix products, arithmetic and copies ran while one was open for 2% of the time, Pallas kernels for 0%

commit v1 on v0

v1 whole, which is shorter than its diff:
```python
import functools

import jax
import jax.numpy as jnp
from jax import lax
from jax.experimental import pallas as pl
from jax.experimental.pallas import tpu as pltpu
from jax.sharding import PartitionSpec as P

HEAD = 128
HEADS = 16
LOW = 4
PARTS = 4
EXCH = 2
CHUNK = 256
MESH = pl.DeviceIdType.MESH
NEG = -1e30
COEF = HEAD**-0.5 * 1.4426950408889634


def flip(value, bits):
    out = value
    bit = 1
    while bit <= bits:
        if bits & bit:
            out = out + bit - 2 * bit * ((value // bit) % 2)
        bit *= 2
    return out


def kernel(
    nreq, nblk,
    q_hbm, ck_hbm, cv_hbm, dk_hbm, dv_hbm, par_ref, len_ref, w_hbm,
    out_hbm,
    qbuf, kbuf, vbuf, dkbuf, dvbuf, vis, nsend, nrecv, ssend, srecv, abuf, wbuf, obuf,
    kv_sem, d_sem, q_send, q_recv, n_send, n_recv, s_send, s_recv,
    wz_send, wx_send, wc_send, w_recv, a_send, a_recv, o_send, o_recv,
):
    batch, own, width = q_hbm.shape
    keys = ck_hbm.shape[1]
    tree = own * nblk
    rows_w, model = w_hbm.shape
    group = 2 * nblk
    ncols = model // group
    depth = nreq // LOW
    req, blk = lax.axis_index("req"), lax.axis_index("blk")
    z, x, c = req // LOW, (req // 2) % 2, req % 2

    def at(zz, xx, cc):
        return zz * LOW + xx * 2 + cc

    part = width // PARTS
    pcols = [pl.ds(p * part, part) for p in range(PARTS)]
    xwidth = width // EXCH
    ecols = [pl.ds(e * xwidth, xwidth) for e in range(EXCH)]

    locals_d = [
        pltpu.make_async_copy(q_hbm, qbuf.at[blk], d_sem.at[0]),
        pltpu.make_async_copy(dk_hbm, dkbuf, d_sem.at[1]),
        pltpu.make_async_copy(dv_hbm, dvbuf, d_sem.at[2]),
    ]
    for copy in locals_d:
        copy.start()
    kv = []
    for p in range(PARTS):
        pair = (
            pltpu.make_async_copy(ck_hbm.at[:, :, pcols[p]], kbuf.at[:, :, pcols[p]], kv_sem.at[0, p]),
            pltpu.make_async_copy(cv_hbm.at[:, :, pcols[p]], vbuf.at[:, :, pcols[p]], kv_sem.at[1, p]),
        )
        for copy in pair:
            copy.start()
        kv.append(pair)

    xpeer, cpeer = at(z, 1 - x, c), at(z, x, 1 - c)
    members = [
        (flip(z, a), lax.rem(blk + b, nblk)) for a in range(2) for b in range(nblk) if a or b
    ]
    peers = [(at(flip(z, d), x, c), blk) for d in range(1, depth)] + [(xpeer, blk), (cpeer, blk)]
    peers += [
        (at(flip(z, a), x, c), lax.rem(blk + b, nblk)) for a in range(2) for b in range(1, nblk)
    ]
    barrier = pltpu.get_barrier_semaphore()
    for peer in peers:
        pl.semaphore_signal(barrier, inc=1, device_id=peer, device_id_type=MESH)
    pl.semaphore_wait(barrier, len(peers))

    def remote(src, dst, send, recv, peer):
        return pltpu.make_async_remote_copy(
            src_ref=src, dst_ref=dst, send_sem=send, recv_sem=recv, device_id=peer, device_id_type=MESH
        )

    sent = []

    def send(*what):
        copy = remote(*what)
        copy.start()
        sent.append(copy)

    def await_recv(dst, sem):
        remote(dst, dst, wz_send.at[0], sem, (xpeer, blk)).wait_recv()

    for b in range(1, nblk):
        send(q_hbm, qbuf.at[blk], q_send.at[b], q_recv.at[blk], (req, lax.rem(blk + b, nblk)))

    def wrows(source):
        return wbuf.at[pl.ds(pl.multiple_of(source * rows_w, rows_w), rows_w)]

    def wsrc(zz):
        index = (zz % 2) * nblk + blk
        return w_hbm.at[:, pl.ds(pl.multiple_of(index * ncols, ncols), ncols)]

    for d in range(1, depth):
        zz = flip(z, d)
        send(wsrc(zz), wrows(req), wz_send.at[d], w_recv.at[req], (at(zz, x, c), blk))
    send(wsrc(z), wrows(req), wx_send.at[0], w_recv.at[req], (xpeer, blk))
    send(wsrc(z), wrows(req), wc_send.at[0], w_recv.at[req], (cpeer, blk))
    own_w = pltpu.make_async_copy(wsrc(z), wrows(req), w_recv.at[req])
    own_w.start()

    def forward_z(d):
        source = at(flip(z, d), x, c)
        await_recv(wrows(source), w_recv.at[source])
        send(wrows(source), wrows(source), wx_send.at[d], w_recv.at[source], (xpeer, blk))
        send(wrows(source), wrows(source), wc_send.at[d], w_recv.at[source], (cpeer, blk))

    def forward_x(d):
        source = at(flip(z, d), 1 - x, c)
        await_recv(wrows(source), w_recv.at[source])
        send(wrows(source), wrows(source), wc_send.at[depth + d], w_recv.at[source], (cpeer, blk))

    row_i = lax.broadcasted_iota(jnp.int32, (tree, tree), 0)
    col_i = lax.broadcasted_iota(jnp.int32, (tree, tree), 1)
    pick = (
        lax.broadcasted_iota(jnp.int32, (tree, own), 0)
        == lax.broadcasted_iota(jnp.int32, (tree, own), 1) + blk * own
    ).astype(jnp.float32).astype(jnp.bfloat16)
    for r in range(batch):
        links = ((par_ref[pl.ds(r, 1), :] == row_i) | (row_i == col_i)).astype(jnp.float32)
        for _ in range((tree - 1).bit_length()):
            half = links.astype(jnp.bfloat16)
            links = jnp.minimum(jnp.dot(half, half, preferred_element_type=jnp.float32), 1.0)
        vis[r] = lax.dot_general(
            links.astype(jnp.bfloat16), pick, (((0,), (0,)), ((), ())),
            preferred_element_type=jnp.float32,
        )
    ssend[...] = jnp.zeros_like(ssend)

    slot = lax.broadcasted_iota(jnp.int32, (1, keys), 1) + blk * keys
    seen = [slot < len_ref[r] for r in range(batch)]
    lane = lax.broadcasted_iota(jnp.int32, (batch * own, 128), 1)
    per_e = HEADS // EXCH

    def head(e, h):
        cols = pl.ds(pl.multiple_of(h * HEAD, HEAD), HEAD)
        stats = []
        for r in range(batch):
            pieces = [qbuf[b, r, :, cols] for b in range(nblk)]
            if own % 16:
                q = jnp.concatenate([piece.astype(jnp.float32) for piece in pieces], axis=0)
                q = q.astype(jnp.bfloat16)
            else:
                q = jnp.concatenate(pieces, axis=0)
            dims = (((1,), (1,)), ((), ()))
            s1 = lax.dot_general(q, kbuf[r, :, cols], dims, preferred_element_type=jnp.float32)
            s2 = lax.dot_general(q, dkbuf[r, :, cols], dims, preferred_element_type=jnp.float32)
            s1 = jnp.where(seen[r], s1, NEG)
            s2 = jnp.where(vis[r] > 0.5, s2, NEG)
            top = jnp.maximum(
                jnp.max(s1, axis=-1, keepdims=True), jnp.max(s2, axis=-1, keepdims=True)
            )
            top = jnp.maximum(top, 0.1 * NEG)
            p1 = jnp.exp2((s1 - top) * COEF)
            p2 = jnp.exp2((s2 - top) * COEF)
            total = jnp.sum(p1, axis=-1, keepdims=True) + jnp.sum(p2, axis=-1, keepdims=True)
            numer = jnp.dot(
                p1.astype(jnp.bfloat16), vbuf[r, :, cols], preferred_element_type=jnp.float32
            ) + jnp.dot(
                p2.astype(jnp.bfloat16), dvbuf[r, :, cols], preferred_element_type=jnp.float32
            )
            stats.append((top, total, numer))
        at_lane = h - e * per_e
        for b in range(nblk):
            rows = slice(b * own, (b + 1) * own)
            top, total, numer = (
                jnp.concatenate([s[i][rows] for s in stats], axis=0) for i in range(3)
            )
            nsend[b, :, cols] = numer.astype(jnp.bfloat16)
            ssend[e, b] = jnp.where(
                lane == at_lane, top, jnp.where(lane == at_lane + 64, total, ssend[e, b])
            )

    def attend(p):
        for copy in kv[p]:
            copy.wait()
        count = HEADS // PARTS
        e = p * EXCH // PARTS

        def body(i, carry):
            head(e, p * count + 2 * i)
            head(e, p * count + 2 * i + 1)
            return carry

        lax.fori_loop(0, count // 2, body, 0)

    def exchange(e):
        for b in range(1, nblk):
            to = lax.rem(blk + b, nblk)
            send(nsend.at[to, :, ecols[e]], nrecv.at[blk, :, ecols[e]], n_send.at[e, b], n_recv.at[e, blk], (req, to))
            send(ssend.at[e, to], srecv.at[e, blk], s_send.at[e, b], s_recv.at[e, blk], (req, to))

    mine = (z % 2) * nblk + blk

    def merge(e):
        stats = [ssend[e, blk]]
        froms = [blk]
        for b in range(1, nblk):
            source = lax.rem(blk + b, nblk)
            await_recv(nrecv.at[source, :, ecols[e]], n_recv.at[e, source])
            await_recv(srecv.at[e, source], s_recv.at[e, source])
            stats.append(srecv[e, source])
            froms.append(source)
        top = functools.reduce(jnp.maximum, stats)
        factors = [jnp.exp2(jnp.minimum((s - top) * COEF, 0.0)) for s in stats]
        total = sum(pltpu.roll(s, 64, 1) * f for s, f in zip(stats, factors))
        factors = [f / total for f in factors]
        for i in range(per_e):
            cols = pl.ds((e * per_e + i) * HEAD, HEAD)
            row = nsend[blk, :, cols].astype(jnp.float32) * factors[0][:, i : i + 1]
            for source, f in zip(froms[1:], factors[1:]):
                row = row + nrecv[source, :, cols].astype(jnp.float32) * f[:, i : i + 1]
            abuf[mine, :, cols] = row.astype(jnp.bfloat16)
        for j, (zz, yy) in enumerate(members):
            block = abuf.at[mine, :, ecols[e]]
            send(block, block, a_send.at[e, j], a_recv.at[e, mine], (at(zz, x, c), yy))

    for copy in locals_d:
        copy.wait()
    for b in range(1, nblk):
        source = lax.rem(blk + b, nblk)
        await_recv(qbuf.at[source], q_recv.at[source])

    attend(0)
    attend(1)
    exchange(0)
    forward_z(1)
    attend(2)
    forward_x(0)
    merge(0)
    forward_z(2)
    attend(3)
    exchange(1)
    forward_x(1)
    for d in range(3, depth):
        forward_z(d)
    merge(1)
    for d in range(2, depth):
        forward_x(d)

    own_w.wait()
    for source in range(depth):
        for low in ((x, 1 - c), (1 - x, 1 - c)):
            index = at(flip(z, source), *low)
            await_recv(wrows(index), w_recv.at[index])
    for e in range(EXCH):
        for zz, yy in members:
            index = (zz % 2) * nblk + yy
            await_recv(abuf.at[index, :, ecols[e]], a_recv.at[e, index])

    homes = []
    for n in range(ncols // CHUNK):
        cols = pl.ds(n * CHUNK, CHUNK)
        mixed = jnp.dot(
            abuf[...].reshape(group * batch * own, width), wbuf[:, cols],
            preferred_element_type=jnp.float32,
        )
        obuf[:, :, :, cols] = mixed.reshape(group, batch, own, CHUNK).astype(jnp.bfloat16)
        there = pl.ds(pl.multiple_of(mine * ncols + n * CHUNK, CHUNK), CHUNK)
        for j, (zz, yy) in enumerate(members):
            index = (zz % 2) * nblk + yy
            send(
                obuf.at[index, :, :, cols], out_hbm.at[:, :, there],
                o_send.at[n, j], o_recv.at[n, mine], (at(zz, x, c), yy),
            )
        home = pltpu.make_async_copy(obuf.at[mine, :, :, cols], out_hbm.at[:, :, there], o_recv.at[n, mine])
        home.start()
        homes.append(home)
    for n in range(ncols // CHUNK):
        homes[n].wait()
        for zz, yy in members:
            index = (zz % 2) * nblk + yy
            there = pl.ds(pl.multiple_of(index * ncols + n * CHUNK, CHUNK), CHUNK)
            await_recv(out_hbm.at[:, :, there], o_recv.at[n, index])
    for copy in sent:
        copy.wait_send()


def shards(nreq, nblk, queries, cache_keys, cache_values, draft_keys, draft_values, parents, lengths, out_weight):
    batch, own, width = queries.shape
    keys = cache_keys.shape[1]
    tree = own * nblk
    rows_w, model = out_weight.shape
    group = 2 * nblk
    ncols = model // group
    depth = nreq // LOW
    bf16, f32 = jnp.bfloat16, jnp.float32
    dma = pltpu.SemaphoreType.DMA
    hbm = pl.BlockSpec(memory_space=pltpu.HBM)
    vmem = pl.BlockSpec(memory_space=pltpu.VMEM)
    smem = pl.BlockSpec(memory_space=pltpu.SMEM)
    pieces = ncols // CHUNK
    return pl.pallas_call(
        functools.partial(kernel, nreq, nblk),
        out_shape=jax.ShapeDtypeStruct((batch, own, model), bf16),
        in_specs=[hbm, hbm, hbm, hbm, hbm, vmem, smem, hbm],
        out_specs=hbm,
        scratch_shapes=[
            pltpu.VMEM((nblk, batch, own, width), bf16),
            pltpu.VMEM((batch, keys, width), bf16),
            pltpu.VMEM((batch, keys, width), bf16),
            pltpu.VMEM((batch, own, width), bf16),
            pltpu.VMEM((batch, own, width), bf16),
            pltpu.VMEM((batch, tree, own), f32),
            pltpu.VMEM((nblk, batch * own, width), bf16),
            pltpu.VMEM((nblk, batch * own, width), bf16),
            pltpu.VMEM((EXCH, nblk, batch * own, 128), f32),
            pltpu.VMEM((EXCH, nblk, batch * own, 128), f32),
            pltpu.VMEM((group, batch * own, width), bf16),
            pltpu.VMEM((rows_w * nreq, ncols), bf16),
            pltpu.VMEM((group, batch, own, ncols), bf16),
            dma((2, PARTS)),
            dma((3,)),
            dma((nblk,)),
            dma((nblk,)),
            dma((EXCH, nblk)),
            dma((EXCH, nblk)),
            dma((EXCH, nblk)),
            dma((EXCH, nblk)),
            dma((depth,)),
            dma((depth,)),
            dma((2 * depth,)),
            dma((nreq,)),
            dma((EXCH, group)),
            dma((EXCH, group)),
            dma((pieces, group)),
            dma((pieces, group)),
        ],
        compiler_params=pltpu.CompilerParams(
            collective_id=0, has_side_effects=True, vmem_limit_bytes=50 * 1024 * 1024
        ),
    )(queries, cache_keys, cache_values, draft_keys, draft_values, parents, lengths, out_weight)


def solution(mesh):
    in_specs = (
        P("req", "blk", None),
        P("req", "blk", None),
        P("req", "blk", None),
        P("req", "blk", None),
        P("req", "blk", None),
        P("req", None),
        P("req"),
        P("req", None),
    )
    out_specs = P("req", "blk", None)
    body = functools.partial(shards, mesh.shape["req"], mesh.shape["blk"])
    return jax.shard_map(body, mesh=mesh, in_specs=in_specs, out_specs=out_specs, check_vma=False)
```

time: 190 us -> 55 us (0.29)
  waiting for transfers between devices: 118 us -> 0 us
  Pallas kernels: 0 us -> 48.5 us
  blocking collectives: 25.7 us -> 0 us
  matrix products: 24.4 us -> 0 us
  between operations: 15 us -> 0.02 us
  local copies, waits for them, and re-layouts: 1.64 us -> 6.2 us
  other arithmetic: 4.35 us -> 0 us
    all_gather x1 -> x0, waiting for transfers between devices: 88.7 us -> none  [shards(): lax.all_gather(out_weight, 'req', axis=0, tiled=True)]
    pallas_call x0 -> x1, Pallas kernels: none -> 48.5 us  [shards(): pl.pallas_call(functools.partial(kernel, nreq, nblk), out_shape=jax.Shape...]
    psum x1 -> x0, waiting for transfers between devices: 29 us -> none  [shards(): summed_numer, summed_totals = lax.psum((numer, totals), 'blk')]
    dot_general x12 -> x0, matrix products: 24.4 us -> none  [the longest x1 9.77 us: shards(): jnp.einsum('rtc,cd->rtd', attended, lax.all_gather(out_weight, 'req', axi...]
    all_gather x1 -> x0, blocking collectives: 10.2 us -> none  [shards(): whole_q = lax.all_gather(queries, 'blk', axis=1, tiled=True)]
    pmax x1 -> x0, blocking collectives: 8.35 us -> none  [shards(): row_max = lax.pmax(local_max, 'blk')]
    psum x1 -> x0, blocking collectives: 7.14 us -> none  [shards(): summed_numer, summed_totals = lax.psum((numer, totals), 'blk')]
    unnamed x2 -> x13, local copies, waits for them, and re-layouts: 0.01 us -> 6.2 us
  transfers between devices with their start and end apart: 2 -> 0, of which waited for: 2 -> 0; matrix products, arithmetic and copies ran while one was open for 2% -> 0% of each run, Pallas kernels for 0% -> 0%
where the time goes in v1:
time: 55 us; the launch traced here: 54.7 us
  Pallas kernels  48.5 us (88%)
  local copies, waits for them, and re-layouts  6.2 us (11%)
    pallas_call x1, Pallas kernels, shards(): pl.pallas_call(functools.partial(kernel, nreq, nblk), out_shape=jax.Shape...  48.5 us
    unnamed x13, local copies, waits for them, and re-layouts  6.2 us

profile of v1, /device:TPU:0, one launch (start us, length us, event | category | flops | bytes accessed | tf_op | source)
XLA Modules:
  0.0 54.7 jit_solution(13556762587913254551)
XLA Ops:
  0.0 0.0 copy-start
  0.0 1.2 %copy-done = bf16[128,4096]{1,0:T(8,128)(2,1)S(1)} copy-done((bf16[128,4096]{1,0:T(8,128)(2,1)S(1)}, bf16[128,4096]{1,0:T(8,128)(2,1)}, u32[]{:S(2)}) %copy-start) | copy-done | bytes 1048600
  1.2 0.0 copy-start.1
  1.2 0.9 %copy-done.1 = bf16[2,32,2048]{2,1,0:T(8,128)(2,1)S(1)} copy-done((bf16[2,32,2048]{2,1,0:T(8,128)(2,1)S(1)}, bf16[2,32,2048]{2,1,0:T(8,128)(2,1)}, u32[]{:S(2)}) %copy-start.1) | copy-done | bytes 262168
  2.2 0.0 copy-start.2
  2.2 0.9 %copy-done.2 = bf16[2,32,2048]{2,1,0:T(8,128)(2,1)S(1)} copy-done((bf16[2,32,2048]{2,1,0:T(8,128)(2,1)S(1)}, bf16[2,32,2048]{2,1,0:T(8,128)(2,1)}, u32[]{:S(2)}) %copy-start.2) | copy-done | bytes 262168
  3.1 0.0 copy-start.3
  3.1 0.9 %copy-done.3 = bf16[2,32,2048]{2,1,0:T(8,128)(2,1)S(1)} copy-done((bf16[2,32,2048]{2,1,0:T(8,128)(2,1)S(1)}, bf16[2,32,2048]{2,1,0:T(8,128)(2,1)}, u32[]{:S(2)}) %copy-start.3) | copy-done | bytes 262168
  4.1 0.0 copy-start.4
  4.1 0.7 %copy-done.4 = s32[2,64]{1,0:T(2,128)S(1)} copy-done((s32[2,64]{1,0:T(2,128)S(1)}, s32[2,64]{1,0:T(2,128)}, u32[]{:S(2)}) %copy-start.4) | copy-done | bytes 536
  4.8 0.0 copy-start.5
  4.8 0.7 %copy-done.5 = s32[2]{0:T(128)S(1)} copy-done((s32[2]{0:T(128)S(1)}, s32[2]{0:T(128)}, u32[]{:S(2)}) %copy-start.5) | copy-done | bytes 32
  5.4 48.5 %shard_map.82 = bf16[2,32,4096]{2,1,0:T(8,128)(2,1)S(1)} custom-call(bf16[2,32,2048]{2,1,0:T(8,128)(2,1)S(1)} %copy-done.1, bf16[2,512,2048]{2,1,0:T(8,128)(2,1)} %ck_hbm.1, bf16[2,512,2048]{2,1,0:T(8,128)(2,1)} %cv_hbm.1, bf16[2,32,2048]{2,1,0:T(8,128)(2,1)S(1)} %copy-done.2, bf16[2,32,2048]{2,1,0:T(8,128)(2,1)S(1)} %copy-done.3, s32[2,64]{1,0:T(2,128)S(1)} %copy-done.4, ...), custom_call_target="tpu_custom_call" | custom-call | tf_op jit(solution)/shard_map/pallas_call | solution.py:311
  53.9 0.8 %copy.10 = bf16[2,32,4096]{2,1,0:T(8,128)(2,1)} copy(bf16[2,32,4096]{2,1,0:T(8,128)(2,1)S(1)} %shard_map.82) | data formatting | bytes 1048576
Async XLA Ops:
  0.0 1.2 %copy-start = (bf16[128,4096]{1,0:T(8,128)(2,1)S(1)}, bf16[128,4096]{1,0:T(8,128)(2,1)}, u32[]{:S(2)}) copy-start(bf16[128,4096]{1,0:T(8,128)(2,1)} %w_hbm.1) | copy-start | bytes 3145732
  1.2 0.9 %copy-start.1 = (bf16[2,32,2048]{2,1,0:T(8,128)(2,1)S(1)}, bf16[2,32,2048]{2,1,0:T(8,128)(2,1)}, u32[]{:S(2)}) copy-start(bf16[2,32,2048]{2,1,0:T(8,128)(2,1)} %q_hbm.1) | copy-start | bytes 786436
  2.2 0.9 %copy-start.2 = (bf16[2,32,2048]{2,1,0:T(8,128)(2,1)S(1)}, bf16[2,32,2048]{2,1,0:T(8,128)(2,1)}, u32[]{:S(2)}) copy-start(bf16[2,32,2048]{2,1,0:T(8,128)(2,1)} %dk_hbm.1) | copy-start | bytes 786436
  3.1 0.9 %copy-start.3 = (bf16[2,32,2048]{2,1,0:T(8,128)(2,1)S(1)}, bf16[2,32,2048]{2,1,0:T(8,128)(2,1)}, u32[]{:S(2)}) copy-start(bf16[2,32,2048]{2,1,0:T(8,128)(2,1)} %dv_hbm.1) | copy-start | bytes 786436
  4.1 0.7 %copy-start.4 = (s32[2,64]{1,0:T(2,128)S(1)}, s32[2,64]{1,0:T(2,128)}, u32[]{:S(2)}) copy-start(s32[2,64]{1,0:T(2,128)} %par_ref.1) | copy-start | bytes 1540
  4.8 0.7 %copy-start.5 = (s32[2]{0:T(128)S(1)}, s32[2]{0:T(128)}, u32[]{:S(2)}) copy-start(s32[2]{0:T(128)} %len_ref.1) | copy-start | bytes 28

commit v2 on v1

--- a/solution.py
+++ b/solution.py
@@ -11,7 +11,6 @@
 HEADS = 16
 LOW = 4
 PARTS = 4
-EXCH = 2
 CHUNK = 256
 MESH = pl.DeviceIdType.MESH
 NEG = -1e30
@@ -32,7 +31,7 @@
     nreq, nblk,
     q_hbm, ck_hbm, cv_hbm, dk_hbm, dv_hbm, par_ref, len_ref, w_hbm,
     out_hbm,
-    qbuf, kbuf, vbuf, dkbuf, dvbuf, vis, nsend, nrecv, ssend, srecv, abuf, wbuf, obuf,
+    qbuf, kbuf, vbuf, dkbuf, dvbuf, vis, nsend, nrecv, stat, ssend, srecv, abuf, wbuf, obuf,
     kv_sem, d_sem, q_send, q_recv, n_send, n_recv, s_send, s_recv,
     wz_send, wx_send, wc_send, w_recv, a_send, a_recv, o_send, o_recv,
 ):
@@ -51,8 +50,6 @@
 
     part = width // PARTS
     pcols = [pl.ds(p * part, part) for p in range(PARTS)]
-    xwidth = width // EXCH
-    ecols = [pl.ds(e * xwidth, xwidth) for e in range(EXCH)]
 
     locals_d = [
         pltpu.make_async_copy(q_hbm, qbuf.at[blk], d_sem.at[0]),
@@ -99,8 +96,12 @@
     def await_recv(dst, sem):
         remote(dst, dst, wz_send.at[0], sem, (xpeer, blk)).wait_recv()
 
-    for b in range(1, nblk):
-        send(q_hbm, qbuf.at[blk], q_send.at[b], q_recv.at[blk], (req, lax.rem(blk + b, nblk)))
+    for p in range(PARTS):
+        for b in range(1, nblk):
+            send(
+                q_hbm.at[:, :, pcols[p]], qbuf.at[blk, :, :, pcols[p]],
+                q_send.at[p, b], q_recv.at[p, blk], (req, lax.rem(blk + b, nblk)),
+            )
 
     def wrows(source):
         return wbuf.at[pl.ds(pl.multiple_of(source * rows_w, rows_w), rows_w)]
@@ -143,14 +144,14 @@
             links.astype(jnp.bfloat16), pick, (((0,), (0,)), ((), ())),
             preferred_element_type=jnp.float32,
         )
-    ssend[...] = jnp.zeros_like(ssend)
+    stat[...] = jnp.zeros_like(stat)
 
     slot = lax.broadcasted_iota(jnp.int32, (1, keys), 1) + blk * keys
     seen = [slot < len_ref[r] for r in range(batch)]
     lane = lax.broadcasted_iota(jnp.int32, (batch * own, 128), 1)
-    per_e = HEADS // EXCH
-
-    def head(e, h):
+    per_p = HEADS // PARTS
+
+    def head(p, h):
         cols = pl.ds(pl.multiple_of(h * HEAD, HEAD), HEAD)
         stats = []
         for r in range(batch):
@@ -178,81 +179,95 @@
                 p2.astype(jnp.bfloat16), dvbuf[r, :, cols], preferred_element_type=jnp.float32
             )
             stats.append((top, total, numer))
-        at_lane = h - e * per_e
+        at_lane = h - p * per_p
         for b in range(nblk):
             rows = slice(b * own, (b + 1) * own)
             top, total, numer = (
                 jnp.concatenate([s[i][rows] for s in stats], axis=0) for i in range(3)
             )
             nsend[b, :, cols] = numer.astype(jnp.bfloat16)
-            ssend[e, b] = jnp.where(
-                lane == at_lane, top, jnp.where(lane == at_lane + 64, total, ssend[e, b])
+            at_rows = pl.ds(b * batch * own, batch * own)
+            stat[p, at_rows] = jnp.where(
+                lane == at_lane, top, jnp.where(lane == at_lane + per_p, total, stat[p, at_rows])
             )
 
     def attend(p):
         for copy in kv[p]:
             copy.wait()
-        count = HEADS // PARTS
-        e = p * EXCH // PARTS
-
-        def body(i, carry):
-            head(e, p * count + 2 * i)
-            head(e, p * count + 2 * i + 1)
-            return carry
-
-        lax.fori_loop(0, count // 2, body, 0)
-
-    def exchange(e):
-        for b in range(1, nblk):
-            to = lax.rem(blk + b, nblk)
-            send(nsend.at[to, :, ecols[e]], nrecv.at[blk, :, ecols[e]], n_send.at[e, b], n_recv.at[e, blk], (req, to))
-            send(ssend.at[e, to], srecv.at[e, blk], s_send.at[e, b], s_recv.at[e, blk], (req, to))
-
-    mine = (z % 2) * nblk + blk
-
-    def merge(e):
-        stats = [ssend[e, blk]]
-        froms = [blk]
         for b in range(1, nblk):
             source = lax.rem(blk + b, nblk)
-            await_recv(nrecv.at[source, :, ecols[e]], n_recv.at[e, source])
-            await_recv(srecv.at[e, source], s_recv.at[e, source])
-            stats.append(srecv[e, source])
-            froms.append(source)
-        top = functools.reduce(jnp.maximum, stats)
-        factors = [jnp.exp2(jnp.minimum((s - top) * COEF, 0.0)) for s in stats]
-        total = sum(pltpu.roll(s, 64, 1) * f for s, f in zip(stats, factors))
+            await_recv(qbuf.at[source, :, :, pcols[p]], q_recv.at[p, source])
+
+        def body(i, carry):
+            head(p, p * per_p + 2 * i)
+            head(p, p * per_p + 2 * i + 1)
+            return carry
+
+        lax.fori_loop(0, per_p // 2, body, 0)
+
+    def exchange(p):
+        ssend[p] = stat[p].T[: 2 * per_p]
+        for b in range(1, nblk):
+            to = (req, lax.rem(blk + b, nblk))
+            send(
+                nsend.at[:, :, pcols[p]], nrecv.at[blk, :, :, pcols[p]],
+                n_send.at[p, b], n_recv.at[p, blk], to,
+            )
+            send(ssend.at[p], srecv.at[p, blk], s_send.at[p, b], s_recv.at[p, blk], to)
+
+    zmod = z % 2
+    mine = zmod * nblk + blk
+    zpeer = (at(flip(z, 1), x, c), blk)
+
+    def tokens(of):
+        return abuf.at[pl.ds(of * nblk, nblk)]
+
+    def merge(p):
+        stats = [stat[p][:, : 2 * per_p]]
+        for b in range(1, nblk):
+            source = lax.rem(blk + b, nblk)
+            await_recv(nrecv.at[source, :, :, pcols[p]], n_recv.at[p, source])
+            await_recv(srecv.at[p, source], s_recv.at[p, source])
+            stats.append(srecv[p, source].T)
+        tops = [s[:, :per_p] for s in stats]
+        sums = [s[:, per_p:] for s in stats]
+        top = functools.reduce(jnp.maximum, tops)
+        factors = [jnp.exp2((t - top) * COEF) for t in tops]
+        total = sum(s * f for s, f in zip(sums, factors))
         factors = [f / total for f in factors]
-        for i in range(per_e):
-            cols = pl.ds((e * per_e + i) * HEAD, HEAD)
-            row = nsend[blk, :, cols].astype(jnp.float32) * factors[0][:, i : i + 1]
-            for source, f in zip(froms[1:], factors[1:]):
-                row = row + nrecv[source, :, cols].astype(jnp.float32) * f[:, i : i + 1]
-            abuf[mine, :, cols] = row.astype(jnp.bfloat16)
-        for j, (zz, yy) in enumerate(members):
-            block = abuf.at[mine, :, ecols[e]]
-            send(block, block, a_send.at[e, j], a_recv.at[e, mine], (at(zz, x, c), yy))
+        for b in range(nblk):
+            rows = slice(b * batch * own, (b + 1) * batch * own)
+            for i in range(per_p):
+                cols = pl.ds((p * per_p + i) * HEAD, HEAD)
+                row = nsend[b, :, cols].astype(jnp.float32) * factors[0][rows, i : i + 1]
+                for a in range(1, nblk):
+                    piece = nrecv[lax.rem(blk + a, nblk), b, :, cols].astype(jnp.float32)
+                    row = row + piece * factors[a][rows, i : i + 1]
+                abuf[zmod * nblk + b, :, cols] = row.astype(jnp.bfloat16)
+        block = tokens(zmod).at[:, :, pcols[p]]
+        send(block, block, a_send.at[p], a_recv.at[p], zpeer)
 
     for copy in locals_d:
         copy.wait()
-    for b in range(1, nblk):
-        source = lax.rem(blk + b, nblk)
-        await_recv(qbuf.at[source], q_recv.at[source])
 
     attend(0)
+    exchange(0)
     attend(1)
-    exchange(0)
+    exchange(1)
     forward_z(1)
-    attend(2)
     forward_x(0)
     merge(0)
+    attend(2)
+    exchange(2)
     forward_z(2)
+    forward_x(1)
+    merge(1)
     attend(3)
-    exchange(1)
-    forward_x(1)
+    exchange(3)
     for d in range(3, depth):
         forward_z(d)
-    merge(1)
+    merge(2)
+    merge(3)
     for d in range(2, depth):
         forward_x(d)
 
@@ -261,10 +276,8 @@
         for low in ((x, 1 - c), (1 - x, 1 - c)):
             index = at(flip(z, source), *low)
             await_recv(wrows(index), w_recv.at[index])
-    for e in range(EXCH):
-        for zz, yy in members:
-            index = (zz % 2) * nblk + yy
-            await_recv(abuf.at[index, :, ecols[e]], a_recv.at[e, index])
+    for p in range(PARTS):
+        await_recv(tokens(1 - zmod).at[:, :, pcols[p]], a_recv.at[p])
 
     homes = []
     for n in range(ncols // CHUNK):
@@ -321,31 +334,32 @@
             pltpu.VMEM((batch, own, width), bf16),
             pltpu.VMEM((batch, tree, own), f32),
             pltpu.VMEM((nblk, batch * own, width), bf16),
-            pltpu.VMEM((nblk, batch * own, width), bf16),
-            pltpu.VMEM((EXCH, nblk, batch * own, 128), f32),
-            pltpu.VMEM((EXCH, nblk, batch * own, 128), f32),
+            pltpu.VMEM((nblk, nblk, batch * own, width), bf16),
+            pltpu.VMEM((PARTS, batch * tree, 128), f32),
+            pltpu.VMEM((PARTS, 2 * HEADS // PARTS, batch * tree), f32),
+            pltpu.VMEM((PARTS, nblk, 2 * HEADS // PARTS, batch * tree), f32),
             pltpu.VMEM((group, batch * own, width), bf16),
             pltpu.VMEM((rows_w * nreq, ncols), bf16),
             pltpu.VMEM((group, batch, own, ncols), bf16),
             dma((2, PARTS)),
             dma((3,)),
-            dma((nblk,)),
-            dma((nblk,)),
-            dma((EXCH, nblk)),
-            dma((EXCH, nblk)),
-            dma((EXCH, nblk)),
-            dma((EXCH, nblk)),
+            dma((PARTS, nblk)),
+            dma((PARTS, nblk)),
+            dma((PARTS, nblk)),
+            dma((PARTS, nblk)),
+            dma((PARTS, nblk)),
+            dma((PARTS, nblk)),
             dma((depth,)),
             dma((depth,)),
             dma((2 * depth,)),
             dma((nreq,)),
-            dma((EXCH, group)),
-            dma((EXCH, group)),
+            dma((PARTS,)),
+            dma((PARTS,)),
             dma((pieces, group)),
             dma((pieces, group)),
         ],
         compiler_params=pltpu.CompilerParams(
-            collective_id=0, has_side_effects=True, vmem_limit_bytes=50 * 1024 * 1024
+            collective_id=0, has_side_effects=True, vmem_limit_bytes=58 * 1024 * 1024
         ),
     )(queries, cache_keys, cache_values, draft_keys, draft_values, parents, lengths, out_weight)
 

time: 55 us -> 50.2 us (0.913)
  local copies, waits for them, and re-layouts: 6.2 us -> 1.87 us
    unnamed x13 -> x1, local copies, waits for them, and re-layouts: 6.2 us -> 1.87 us
where the time goes in v2:
time: 50.2 us; the launch traced here: 50 us
  Pallas kernels  48.1 us (96%)
  local copies, waits for them, and re-layouts  1.87 us (4%)
    pallas_call x1, Pallas kernels, shards(): pl.pallas_call(functools.partial(kernel, nreq, nblk), out_shape=jax.Shape...  48.1 us
    unnamed x1, local copies, waits for them, and re-layouts  1.87 us

profile of v2, /device:TPU:0, one launch (start us, length us, event | category | flops | bytes accessed | tf_op | source)
XLA Modules:
  0.0 50.0 jit_solution(18433656316005817359)
XLA Ops:
  0.0 48.1 %shard_map.82 = bf16[2,32,4096]{2,1,0:T(8,128)(2,1)} custom-call(bf16[2,32,2048]{2,1,0:T(8,128)(2,1)} %q_hbm.1, bf16[2,512,2048]{2,1,0:T(8,128)(2,1)} %ck_hbm.1, bf16[2,512,2048]{2,1,0:T(8,128)(2,1)} %cv_hbm.1, bf16[2,32,2048]{2,1,0:T(8,128)(2,1)} %dk_hbm.1, bf16[2,32,2048]{2,1,0:T(8,128)(2,1)} %dv_hbm.1, s32[2,64]{1,0:T(2,128)} %par_ref.1, s32[2]{0:T(128)} %len_ref.1, ...), custom_call_target="tpu_custom_call" | custom-call | tf_op jit(solution)/shard_map/pallas_call | solution.py:324
  48.1 1.9 %copy.10 = bf16[2,32,4096]{2,1,0:T(8,128)(2,1)} copy(bf16[2,32,4096]{2,1,0:T(8,128)(2,1)} %shard_map.82) | data formatting | bytes 1048576
